TPU v7x, 32 devices: a whole 2x2x4 slice. The times are simulated.
32 devices in a mesh: layer: 8 (over z, core), dp: 4 (over y, x).
Axes of the slice: x: 2, y: 2, z: 4, core: 2. Of those that a mesh axis runs over, the one named last changes fastest.
Arguments:
- starts: float32 [8, 4, 32, 32, 128], P('layer', 'dp'), may hold values from -6 to 6
- weights: bfloat16 [32, 9, 128, 128], P('layer'), may hold values from -0.1875 to 0.1875
- biases: bfloat16 [32, 128], P('layer'), may hold values from -3 to 3
- adj_ends: float32 [8, 4, 32, 32, 128], P('layer', 'dp'), may hold values from -6 to 6
Outputs:
- block_ends: float32 [8, 4, 32, 32, 128], P('layer', 'dp')
- adjoint_starts: float32 [8, 4, 32, 32, 128], P('layer', 'dp')
- weight_grad: float32 [32, 9, 128, 128], P('layer')
- bias_grad: float32 [32, 128], P('layer')
All inputs are finite; a program needn't handle non-finite values.
Results may differ from a plain program's by a relative error of at most 0.039.
Values may be sent and summed in bfloat16 or wider, within the bound.
A program may use at most 64 MiB of HBM per device.

v0:
```python
import math

import jax
import jax.numpy as jnp
from jax import lax
from jax.sharding import PartitionSpec as P

step_size = 0.25


def passed_along(x, axis, by):
    peers = lax.axis_size(axis)
    pairs = [(i, i + by) for i in range(peers) if 0 <= i + by < peers]
    return lax.ppermute(x, axis, pairs)


def convolve(rounded, kernel):
    count, map_side, _, channels = rounded.shape
    padded = jnp.pad(rounded, ((0, 0), (1, 1), (1, 1), (0, 0)))
    running = jnp.zeros((count * map_side * map_side, kernel.shape[2]), jnp.float32)
    for tap_index in range(9):
        row_off = tap_index // 3
        col_off = tap_index % 3
        view = padded[:, row_off : row_off + map_side, col_off : col_off + map_side, :].reshape(
            count * map_side * map_side, channels
        )
        running = running + jnp.dot(view, kernel[tap_index], preferred_element_type=jnp.float32)
    return running.reshape(count, map_side, map_side, kernel.shape[2])


def transposed(signal, kernel):
    count, map_side, _, channels = signal.shape
    padded = jnp.pad(signal, ((0, 0), (1, 1), (1, 1), (0, 0)))
    running = jnp.zeros((count * map_side * map_side, kernel.shape[1]), jnp.float32)
    for tap_index in range(9):
        row_off = 2 - tap_index // 3
        col_off = 2 - tap_index % 3
        view = padded[:, row_off : row_off + map_side, col_off : col_off + map_side, :].reshape(
            count * map_side * map_side, channels
        )
        running = running + lax.dot_general(
            view, kernel[tap_index], (((1,), (1,)), ((), ())), preferred_element_type=jnp.float32
        )
    return running.reshape(count, map_side, map_side, kernel.shape[1])


def correlate(rounded, signal):
    count, map_side, _, channels = rounded.shape
    padded = jnp.pad(rounded, ((0, 0), (1, 1), (1, 1), (0, 0)))
    flat_signal = signal.reshape(count * map_side * map_side, signal.shape[3])
    pieces = []
    for tap_index in range(9):
        row_off = tap_index // 3
        col_off = tap_index % 3
        view = padded[:, row_off : row_off + map_side, col_off : col_off + map_side, :].reshape(
            count * map_side * map_side, channels
        )
        pieces.append(
            lax.dot_general(
                view, flat_signal, (((0,), (0,)), ((), ())), preferred_element_type=jnp.float32
            )
        )
    return jnp.stack(pieces)


def activation_of(rounded, kernel, bias_row):
    return jnp.tanh(convolve(rounded, kernel) + bias_row.astype(jnp.float32))


def local(starts, weights, biases, adj_ends):
    layer_index = lax.axis_index("layer")
    blocks = lax.axis_size("layer")
    block_depth = weights.shape[0]
    coarse_step = block_depth * step_size
    map_side = starts.shape[2]
    image_total = starts.shape[1] * lax.axis_size("dp")
    grad_scale = 1.0 / (map_side * math.sqrt(image_total))
    first_state = starts[0]
    adjoint_guess = adj_ends[0]
    first_kernel = weights[0]
    first_bias = biases[0]

    def coarse_apply(current_state, kernel, bias_row):
        return current_state + coarse_step * activation_of(
            current_state.astype(jnp.bfloat16), kernel, bias_row
        )

    current_state = first_state
    for inner_pos in range(block_depth):
        current_state = current_state + step_size * activation_of(
            current_state.astype(jnp.bfloat16), weights[inner_pos], biases[inner_pos]
        )
    relaxed = current_state
    offset = relaxed - coarse_apply(first_state, first_kernel, first_bias)

    def advance(step_index, carried):
        produced = lax.cond(
            layer_index == step_index,
            lambda held: offset + coarse_apply(held, first_kernel, first_bias),
            lambda held: jnp.zeros_like(held),
            carried,
        )
        received = passed_along(produced, "layer", 1)
        return jnp.where(layer_index == step_index + 1, received, carried)

    entry = lax.fori_loop(0, blocks - 1, advance, first_state)
    saved_states = []
    saved_slopes = []
    current_state = entry
    for inner_pos in range(block_depth):
        rounded = current_state.astype(jnp.bfloat16)
        saved_states.append(rounded)
        activation = activation_of(rounded, weights[inner_pos], biases[inner_pos])
        saved_slopes.append(1.0 - activation * activation)
        current_state = current_state + step_size * activation
    adjoint = adjoint_guess
    for inner_pos in reversed(range(block_depth)):
        signal = (saved_slopes[inner_pos] * adjoint).astype(jnp.bfloat16)
        adjoint = adjoint + step_size * transposed(signal, weights[inner_pos])
    backed = adjoint

    def coarse_adjoint(difference):
        signal = (saved_slopes[0] * difference).astype(jnp.bfloat16)
        return difference + coarse_step * transposed(signal, first_kernel)

    def retreat(step_index, carried):
        sender = blocks - 1 - step_index
        produced = lax.cond(
            layer_index == sender,
            lambda held: backed + coarse_adjoint(held - adjoint_guess),
            lambda held: jnp.zeros_like(held),
            carried,
        )
        received = passed_along(produced.astype(jnp.bfloat16), "layer", -1).astype(produced.dtype)
        return jnp.where(layer_index == sender - 1, received, carried)

    exit_adjoint = lax.fori_loop(0, blocks - 1, retreat, adjoint_guess)
    kernel_grads = [None] * block_depth
    bias_grads = [None] * block_depth
    adjoint = exit_adjoint
    for inner_pos in reversed(range(block_depth)):
        signal = (saved_slopes[inner_pos] * adjoint).astype(jnp.bfloat16)
        kernel_part = correlate(saved_states[inner_pos], signal) * grad_scale
        bias_part = jnp.sum(signal.astype(jnp.float32), axis=(0, 1, 2)) * grad_scale
        kernel_grads[inner_pos] = kernel_part
        bias_grads[inner_pos] = bias_part
        adjoint = adjoint + step_size * transposed(signal, weights[inner_pos])
    kernel_stack = jnp.stack(kernel_grads)
    bias_stack = jnp.stack(bias_grads)
    kernel_stack, bias_stack = (
        lax.psum(kernel_stack.astype(jnp.bfloat16), "dp").astype(jnp.float32),
        lax.psum(bias_stack.astype(jnp.bfloat16), "dp").astype(jnp.float32),
    )
    return (current_state[None], adjoint[None], kernel_stack, bias_stack)


def solution(mesh):
    in_specs = (
        P("layer", "dp", None, None, None),
        P("layer", None, None, None),
        P("layer", None),
        P("layer", "dp", None, None, None),
    )
    out_specs = (
        P("layer", "dp", None, None, None),
        P("layer", "dp", None, None, None),
        P("layer", None, None, None),
        P("layer", None),
    )
    return jax.shard_map(local, mesh=mesh, in_specs=in_specs, out_specs=out_specs, check_vma=False)
```

profile of v0, /device:TPU:0, one launch (start us, length us, event | category | flops | bytes accessed | tf_op | source)
XLA Modules:
  0.0 288.4 jit_solution(2083467606569354930)
XLA Ops:
  7.2 1.0 copy.59
  8.7 0.9 copy-done.1
  17.1 1.1 pad_slice_fusion.112
  19.4 1.2 convolution_add_fusion.115
  22.3 78.4 %while.30 = (s32[]{:T(128)}, f32[1,32,32,128]{3,2,1,0:T(8,128)S(1)}, s32[]{:T(128)}, bf16[9,128,128]{2,1,0:T(8,128)(2,1)S(1)}, bf16[128]{0:T(256)(128)(2,1)S(1)}, /*index=5*/f32[1,32,32,128]{3,2,1,0:T(8,128)S(1)}, s32[]{:T(128)}) while((s32[]{:T(128)}, f32[1,32,32,128]{3,2,1,0:T(8,128)S(1)}, s32[]{:T(128)}, ...), condition=%wide.region_3.4_spmd, body=%wide.region_0.3_spmd.sunk | while | flops 303693952 | bytes 22578640 | solution.py:106
  22.4 2.5 conditional.4
  25.6 1.3 collective-permute-start
  27.0 1.7 collective-permute-done
  28.9 0.8 copy-done.5
  29.7 10.3 %collective-permute-start = (f32[1,32,32,128]{3,2,1,0:T(8,128)}, f32[1,32,32,128]{3,2,1,0:T(8,128)S(1)}, u32[]{:S(2)}, u32[]{:S(2)}) collective-permute-start(f32[1,32,32,128]{3,2,1,0:T(8,128)} %copy-done.5), channel_id=1, source_target_pairs={{0,4},{4,8},{8,12},{12,16},{16,20},{20,24},{24,28},{1,5},{5,9},{9,... | collective-permute-start | bytes 1572872 | tf_op jit(solution)/shard_map/while/body/eval_jaxpr/ppermute | solution.py:14
  40.0 1.7 collective-permute-done
  42.8 6.6 %collective-permute-start = (f32[1,32,32,128]{3,2,1,0:T(8,128)}, f32[1,32,32,128]{3,2,1,0:T(8,128)S(1)}, u32[]{:S(2)}, u32[]{:S(2)}) collective-permute-start(f32[1,32,32,128]{3,2,1,0:T(8,128)} %copy-done.5), channel_id=1, source_target_pairs={{0,4},{4,8},{8,12},{12,16},{16,20},{20,24},{24,28},{1,5},{5,9},{9,... | collective-permute-start | bytes 1572872 | tf_op jit(solution)/shard_map/while/body/eval_jaxpr/ppermute | solution.py:14
  49.4 1.7 collective-permute-done
  52.1 11.4 %collective-permute-start = (f32[1,32,32,128]{3,2,1,0:T(8,128)}, f32[1,32,32,128]{3,2,1,0:T(8,128)S(1)}, u32[]{:S(2)}, u32[]{:S(2)}) collective-permute-start(f32[1,32,32,128]{3,2,1,0:T(8,128)} %copy-done.5), channel_id=1, source_target_pairs={{0,4},{4,8},{8,12},{12,16},{16,20},{20,24},{24,28},{1,5},{5,9},{9,... | collective-permute-start | bytes 1572872 | tf_op jit(solution)/shard_map/while/body/eval_jaxpr/ppermute | solution.py:14
  63.5 1.7 collective-permute-done
  66.3 9.0 %collective-permute-start = (f32[1,32,32,128]{3,2,1,0:T(8,128)}, f32[1,32,32,128]{3,2,1,0:T(8,128)S(1)}, u32[]{:S(2)}, u32[]{:S(2)}) collective-permute-start(f32[1,32,32,128]{3,2,1,0:T(8,128)} %copy-done.5), channel_id=1, source_target_pairs={{0,4},{4,8},{8,12},{12,16},{16,20},{20,24},{24,28},{1,5},{5,9},{9,... | collective-permute-start | bytes 1572872 | tf_op jit(solution)/shard_map/while/body/eval_jaxpr/ppermute | solution.py:14
  75.3 1.7 collective-permute-done
  77.2 0.8 copy-done.5
  78.0 9.0 %collective-permute-start = (f32[1,32,32,128]{3,2,1,0:T(8,128)}, f32[1,32,32,128]{3,2,1,0:T(8,128)S(1)}, u32[]{:S(2)}, u32[]{:S(2)}) collective-permute-start(f32[1,32,32,128]{3,2,1,0:T(8,128)} %copy-done.5), channel_id=1, source_target_pairs={{0,4},{4,8},{8,12},{12,16},{16,20},{20,24},{24,28},{1,5},{5,9},{9,... | collective-permute-start | bytes 1572872 | tf_op jit(solution)/shard_map/while/body/eval_jaxpr/ppermute | solution.py:14
  87.0 1.7 collective-permute-done
  88.9 0.8 copy-done.5
  89.7 9.0 %collective-permute-start = (f32[1,32,32,128]{3,2,1,0:T(8,128)}, f32[1,32,32,128]{3,2,1,0:T(8,128)S(1)}, u32[]{:S(2)}, u32[]{:S(2)}) collective-permute-start(f32[1,32,32,128]{3,2,1,0:T(8,128)} %copy-done.5), channel_id=1, source_target_pairs={{0,4},{4,8},{8,12},{12,16},{16,20},{20,24},{24,28},{1,5},{5,9},{9,... | collective-permute-start | bytes 1572872 | tf_op jit(solution)/shard_map/while/body/eval_jaxpr/ppermute | solution.py:14
  98.7 1.7 collective-permute-done
  122.7 0.9 add.1103
  123.5 73.3 %while.31 = (s32[]{:T(128)}, f32[1,32,32,128]{3,2,1,0:T(8,128)S(1)}, s32[]{:T(128)}, f32[1,32,32,128]{3,2,1,0:T(8,128)S(1)}, f32[1,32,32,128]{3,2,1,0:T(8,128)S(...) while((s32[]{:T(128)}, ...), condition=%wide.region_7.8_spmd, body=%wide.region_4.7_spmd.sunk | while | flops 304087040 | bytes 23626020 | solution.py:137
  124.3 1.3 collective-permute-start.1
  125.6 8.9 %collective-permute-done.1 = bf16[1,32,32,128]{3,2,1,0:T(8,128)(2,1)S(1)} collective-permute-done((bf16[1,32,32,128]{3,2,1,0:T(8,128)(2,1)}, bf16[1,32,32,128]{3,2,1,0:T(8,128)(2,1)S(1)}, u32[]{:S(2)}, u32[]{:S(2)}) %collective-permute-start.1) | collective-permute-done | bytes 262176 | tf_op jit(solution)/shard_map/while/body/eval_jaxpr/ppermute | solution.py:14
  135.4 1.3 collective-permute-start.1
  136.7 7.2 %collective-permute-done.1 = bf16[1,32,32,128]{3,2,1,0:T(8,128)(2,1)S(1)} collective-permute-done((bf16[1,32,32,128]{3,2,1,0:T(8,128)(2,1)}, bf16[1,32,32,128]{3,2,1,0:T(8,128)(2,1)S(1)}, u32[]{:S(2)}, u32[]{:S(2)}) %collective-permute-start.1) | collective-permute-done | bytes 262176 | tf_op jit(solution)/shard_map/while/body/eval_jaxpr/ppermute | solution.py:14
  144.9 1.3 collective-permute-start.1
  146.2 6.6 %collective-permute-done.1 = bf16[1,32,32,128]{3,2,1,0:T(8,128)(2,1)S(1)} collective-permute-done((bf16[1,32,32,128]{3,2,1,0:T(8,128)(2,1)}, bf16[1,32,32,128]{3,2,1,0:T(8,128)(2,1)S(1)}, u32[]{:S(2)}, u32[]{:S(2)}) %collective-permute-start.1) | collective-permute-done | bytes 262176 | tf_op jit(solution)/shard_map/while/body/eval_jaxpr/ppermute | solution.py:14
  153.7 1.3 collective-permute-start.1
  155.0 6.6 %collective-permute-done.1 = bf16[1,32,32,128]{3,2,1,0:T(8,128)(2,1)S(1)} collective-permute-done((bf16[1,32,32,128]{3,2,1,0:T(8,128)(2,1)}, bf16[1,32,32,128]{3,2,1,0:T(8,128)(2,1)S(1)}, u32[]{:S(2)}, u32[]{:S(2)}) %collective-permute-start.1) | collective-permute-done | bytes 262176 | tf_op jit(solution)/shard_map/while/body/eval_jaxpr/ppermute | solution.py:14
  162.5 1.3 collective-permute-start.1
  163.8 6.6 %collective-permute-done.1 = bf16[1,32,32,128]{3,2,1,0:T(8,128)(2,1)S(1)} collective-permute-done((bf16[1,32,32,128]{3,2,1,0:T(8,128)(2,1)}, bf16[1,32,32,128]{3,2,1,0:T(8,128)(2,1)S(1)}, u32[]{:S(2)}, u32[]{:S(2)}) %collective-permute-start.1) | collective-permute-done | bytes 262176 | tf_op jit(solution)/shard_map/while/body/eval_jaxpr/ppermute | solution.py:14
  171.4 1.3 collective-permute-start.1
  172.7 6.6 %collective-permute-done.1 = bf16[1,32,32,128]{3,2,1,0:T(8,128)(2,1)S(1)} collective-permute-done((bf16[1,32,32,128]{3,2,1,0:T(8,128)(2,1)}, bf16[1,32,32,128]{3,2,1,0:T(8,128)(2,1)S(1)}, u32[]{:S(2)}, u32[]{:S(2)}) %collective-permute-start.1) | collective-permute-done | bytes 262176 | tf_op jit(solution)/shard_map/while/body/eval_jaxpr/ppermute | solution.py:14
  180.2 1.3 collective-permute-start.1
  181.5 15.0 %collective-permute-done.1 = bf16[1,32,32,128]{3,2,1,0:T(8,128)(2,1)S(1)} collective-permute-done((bf16[1,32,32,128]{3,2,1,0:T(8,128)(2,1)}, bf16[1,32,32,128]{3,2,1,0:T(8,128)(2,1)S(1)}, u32[]{:S(2)}, u32[]{:S(2)}) %collective-permute-start.1) | collective-permute-done | bytes 262176 | tf_op jit(solution)/shard_map/while/body/eval_jaxpr/ppermute | solution.py:14
  196.8 1.2 convert_reduce_fusion
  201.3 1.1 convert_reduce_fusion.1
  220.1 1.2 pad_maximum_fusion
  221.3 1.3 pad_slice_fusion.16
  222.6 10.0 %psum.15 = bf16[4,128]{1,0:T(4,128)(2,1)S(1)} all-reduce(bf16[4,128]{1,0:T(4,128)(2,1)S(1)} %pad_maximum_fusion.1), channel_id=1, replica_groups=mesh['layer'=8,'dp'=4] {'dp'}, use_global_device_ids=true, to_apply=%region_13.14 | all-reduce | flops 512 | bytes 2048 | tf_op jit(solution)/shard_map/psum | solution.py:152
  233.4 1.2 convolution_add_fusion.23
  237.3 0.9 add_bitcast_fusion
  238.2 40.4 %all-reduce.20.cloned.1.call-done = bf16[4,9,128,128]{3,2,1,0:T(8,128)(2,1)} async-done(((bf16[4,9,128,128]{3,2,1,0:T(8,128)(2,1)}), bf16[4,9,128,128]{3,2,1,0:T(8,128)(2,1)}) %all-reduce.20.cloned.1.call-update) | async-done | bytes 1179664 | tf_op jit(solution)/shard_map/psum | solution.py:151
  278.6 3.0 %convert_element_type.313 = f32[4,9,128,128]{3,2,1,0:T(8,128)} convert(bf16[4,9,128,128]{3,2,1,0:T(8,128)(2,1)} %all-reduce.20.cloned.1.call-done) | non-fusion elementwise | flops 589824 | bytes 3538944 | tf_op jit(solution)/shard_map/convert_element_type | solution.py:151
  (354 shorter events, 69.2 us)
Async XLA Ops:
  7.2 271.5 %all-reduce.20.cloned.1.call-start = ((), (), s32[]{:S(2)}) async-start(), calls=%async_computation | async-start | bytes 2359296 | tf_op jit(solution)/shard_map/psum | solution.py:151
  8.3 1.3 copy-start.1
  12.1 2.4 copy-start.10
  14.7 2.3 copy-start.15
  19.3 1.2 copy-start.31
  19.4 1.5 copy-start.29
  20.8 1.0 copy-start.11
  20.8 1.2 copy-start.16
  24.8 0.8 copy-start.5
  25.6 3.0 %collective-permute-start = (f32[1,32,32,128]{3,2,1,0:T(8,128)}, f32[1,32,32,128]{3,2,1,0:T(8,128)S(1)}, u32[]{:S(2)}, u32[]{:S(2)}) collective-permute-start(f32[1,32,32,128]{3,2,1,0:T(8,128)} %copy-done.5), channel_id=1, source_target_pairs={{0,4},{4,8},{8,12},{12,16},{16,20},{20,24},{24,28},{1,5},{5,9},{9,... | collective-permute-start | bytes 1572872 | tf_op jit(solution)/shard_map/while/body/eval_jaxpr/ppermute | solution.py:14
  28.9 0.8 copy-start.5
  29.7 12.0 %collective-permute-start = (f32[1,32,32,128]{3,2,1,0:T(8,128)}, f32[1,32,32,128]{3,2,1,0:T(8,128)S(1)}, u32[]{:S(2)}, u32[]{:S(2)}) collective-permute-start(f32[1,32,32,128]{3,2,1,0:T(8,128)} %copy-done.5), channel_id=1, source_target_pairs={{0,4},{4,8},{8,12},{12,16},{16,20},{20,24},{24,28},{1,5},{5,9},{9,... | collective-permute-start | bytes 1572872 | tf_op jit(solution)/shard_map/while/body/eval_jaxpr/ppermute | solution.py:14
  42.0 0.8 copy-start.5
  42.8 8.3 %collective-permute-start = (f32[1,32,32,128]{3,2,1,0:T(8,128)}, f32[1,32,32,128]{3,2,1,0:T(8,128)S(1)}, u32[]{:S(2)}, u32[]{:S(2)}) collective-permute-start(f32[1,32,32,128]{3,2,1,0:T(8,128)} %copy-done.5), channel_id=1, source_target_pairs={{0,4},{4,8},{8,12},{12,16},{16,20},{20,24},{24,28},{1,5},{5,9},{9,... | collective-permute-start | bytes 1572872 | tf_op jit(solution)/shard_map/while/body/eval_jaxpr/ppermute | solution.py:14
  52.1 13.1 %collective-permute-start = (f32[1,32,32,128]{3,2,1,0:T(8,128)}, f32[1,32,32,128]{3,2,1,0:T(8,128)S(1)}, u32[]{:S(2)}, u32[]{:S(2)}) collective-permute-start(f32[1,32,32,128]{3,2,1,0:T(8,128)} %copy-done.5), channel_id=1, source_target_pairs={{0,4},{4,8},{8,12},{12,16},{16,20},{20,24},{24,28},{1,5},{5,9},{9,... | collective-permute-start | bytes 1572872 | tf_op jit(solution)/shard_map/while/body/eval_jaxpr/ppermute | solution.py:14
  66.3 10.7 %collective-permute-start = (f32[1,32,32,128]{3,2,1,0:T(8,128)}, f32[1,32,32,128]{3,2,1,0:T(8,128)S(1)}, u32[]{:S(2)}, u32[]{:S(2)}) collective-permute-start(f32[1,32,32,128]{3,2,1,0:T(8,128)} %copy-done.5), channel_id=1, source_target_pairs={{0,4},{4,8},{8,12},{12,16},{16,20},{20,24},{24,28},{1,5},{5,9},{9,... | collective-permute-start | bytes 1572872 | tf_op jit(solution)/shard_map/while/body/eval_jaxpr/ppermute | solution.py:14
  77.2 0.8 copy-start.5
  78.0 10.7 %collective-permute-start = (f32[1,32,32,128]{3,2,1,0:T(8,128)}, f32[1,32,32,128]{3,2,1,0:T(8,128)S(1)}, u32[]{:S(2)}, u32[]{:S(2)}) collective-permute-start(f32[1,32,32,128]{3,2,1,0:T(8,128)} %copy-done.5), channel_id=1, source_target_pairs={{0,4},{4,8},{8,12},{12,16},{16,20},{20,24},{24,28},{1,5},{5,9},{9,... | collective-permute-start | bytes 1572872 | tf_op jit(solution)/shard_map/while/body/eval_jaxpr/ppermute | solution.py:14
  88.9 0.8 copy-start.5
  89.7 10.7 %collective-permute-start = (f32[1,32,32,128]{3,2,1,0:T(8,128)}, f32[1,32,32,128]{3,2,1,0:T(8,128)S(1)}, u32[]{:S(2)}, u32[]{:S(2)}) collective-permute-start(f32[1,32,32,128]{3,2,1,0:T(8,128)} %copy-done.5), channel_id=1, source_target_pairs={{0,4},{4,8},{8,12},{12,16},{16,20},{20,24},{24,28},{1,5},{5,9},{9,... | collective-permute-start | bytes 1572872 | tf_op jit(solution)/shard_map/while/body/eval_jaxpr/ppermute | solution.py:14
  100.8 1.2 copy-start.17
  103.2 1.2 copy-start.19
  105.5 13.2 %copy-start.6 = (f32[1024,128]{1,0:T(8,128)}, f32[1024,128]{1,0:T(8,128)S(1)}, u32[]{:S(2)}) copy-start(f32[1024,128]{1,0:T(8,128)S(1)} %convolution_add_fusion.96) | copy-start | bytes 1572868
  105.7 1.2 copy-start.21
  105.7 2.3 copy-start.13
  108.0 7.9 %copy-start.3 = (f32[1024,128]{1,0:T(8,128)}, f32[1024,128]{1,0:T(8,128)S(1)}, u32[]{:S(2)}) copy-start(f32[1024,128]{1,0:T(8,128)S(1)} %convolution_add_fusion.88) | copy-start | bytes 1572868
  108.1 1.2 copy-start.23
  109.7 1.0 copy-start
  124.3 10.2 %collective-permute-start.1 = (bf16[1,32,32,128]{3,2,1,0:T(8,128)(2,1)}, bf16[1,32,32,128]{3,2,1,0:T(8,128)(2,1)S(1)}, u32[]{:S(2)}, u32[]{:S(2)}) collective-permute-start(bf16[1,32,32,128]{3,2,1,0:T(8,128)(2,1)} %copy-done.12), channel_id=1, source_target_pairs={{4,0},{8,4},{12,8},{16,12},{20,16},{24,20},{28,24},{5,1},{9,5},{13... | collective-permute-start | bytes 786440 | tf_op jit(solution)/shard_map/while/body/eval_jaxpr/ppermute | solution.py:14
  135.4 8.5 %collective-permute-start.1 = (bf16[1,32,32,128]{3,2,1,0:T(8,128)(2,1)}, bf16[1,32,32,128]{3,2,1,0:T(8,128)(2,1)S(1)}, u32[]{:S(2)}, u32[]{:S(2)}) collective-permute-start(bf16[1,32,32,128]{3,2,1,0:T(8,128)(2,1)} %copy-done.12), channel_id=1, source_target_pairs={{4,0},{8,4},{12,8},{16,12},{20,16},{24,20},{28,24},{5,1},{9,5},{13... | collective-permute-start | bytes 786440 | tf_op jit(solution)/shard_map/while/body/eval_jaxpr/ppermute | solution.py:14
  144.9 7.9 %collective-permute-start.1 = (bf16[1,32,32,128]{3,2,1,0:T(8,128)(2,1)}, bf16[1,32,32,128]{3,2,1,0:T(8,128)(2,1)S(1)}, u32[]{:S(2)}, u32[]{:S(2)}) collective-permute-start(bf16[1,32,32,128]{3,2,1,0:T(8,128)(2,1)} %copy-done.12), channel_id=1, source_target_pairs={{4,0},{8,4},{12,8},{16,12},{20,16},{24,20},{28,24},{5,1},{9,5},{13... | collective-permute-start | bytes 786440 | tf_op jit(solution)/shard_map/while/body/eval_jaxpr/ppermute | solution.py:14
  153.7 7.9 %collective-permute-start.1 = (bf16[1,32,32,128]{3,2,1,0:T(8,128)(2,1)}, bf16[1,32,32,128]{3,2,1,0:T(8,128)(2,1)S(1)}, u32[]{:S(2)}, u32[]{:S(2)}) collective-permute-start(bf16[1,32,32,128]{3,2,1,0:T(8,128)(2,1)} %copy-done.12), channel_id=1, source_target_pairs={{4,0},{8,4},{12,8},{16,12},{20,16},{24,20},{28,24},{5,1},{9,5},{13... | collective-permute-start | bytes 786440 | tf_op jit(solution)/shard_map/while/body/eval_jaxpr/ppermute | solution.py:14
  162.5 7.9 %collective-permute-start.1 = (bf16[1,32,32,128]{3,2,1,0:T(8,128)(2,1)}, bf16[1,32,32,128]{3,2,1,0:T(8,128)(2,1)S(1)}, u32[]{:S(2)}, u32[]{:S(2)}) collective-permute-start(bf16[1,32,32,128]{3,2,1,0:T(8,128)(2,1)} %copy-done.12), channel_id=1, source_target_pairs={{4,0},{8,4},{12,8},{16,12},{20,16},{24,20},{28,24},{5,1},{9,5},{13... | collective-permute-start | bytes 786440 | tf_op jit(solution)/shard_map/while/body/eval_jaxpr/ppermute | solution.py:14
  171.4 7.9 %collective-permute-start.1 = (bf16[1,32,32,128]{3,2,1,0:T(8,128)(2,1)}, bf16[1,32,32,128]{3,2,1,0:T(8,128)(2,1)S(1)}, u32[]{:S(2)}, u32[]{:S(2)}) collective-permute-start(bf16[1,32,32,128]{3,2,1,0:T(8,128)(2,1)} %copy-done.12), channel_id=1, source_target_pairs={{4,0},{8,4},{12,8},{16,12},{20,16},{24,20},{28,24},{5,1},{9,5},{13... | collective-permute-start | bytes 786440 | tf_op jit(solution)/shard_map/while/body/eval_jaxpr/ppermute | solution.py:14
  180.2 16.3 %collective-permute-start.1 = (bf16[1,32,32,128]{3,2,1,0:T(8,128)(2,1)}, bf16[1,32,32,128]{3,2,1,0:T(8,128)(2,1)S(1)}, u32[]{:S(2)}, u32[]{:S(2)}) collective-permute-start(bf16[1,32,32,128]{3,2,1,0:T(8,128)(2,1)} %copy-done.12), channel_id=1, source_target_pairs={{4,0},{8,4},{12,8},{16,12},{20,16},{24,20},{28,24},{5,1},{9,5},{13... | collective-permute-start | bytes 786440 | tf_op jit(solution)/shard_map/while/body/eval_jaxpr/ppermute | solution.py:14
  200.0 1.0 copy-start.4
  200.0 1.2 copy-start.9
  200.0 1.3 copy-start.14
  204.4 1.0 copy-start.7
  205.7 0.9 copy-start.20
  205.7 1.2 copy-start.22
  206.6 1.0 copy-start.24
  209.7 1.0 copy-start.18
  232.6 2.0 copy-start.30
  233.4 1.5 copy-start.28
  234.9 1.0 copy-start.27
  235.1 1.0 copy-start.26
  235.8 1.0 copy-start.25
  (11 other events, 8.1 us)
Sparse Core Ops, SparseCore 0:
  221.4 57.1 all-reduce.19
where the time goes:
time: 289 us; the launch traced here: 288 us
  waiting for transfers between devices  110 us (38%)
  starting transfers between devices  65.7 us (23%)
  matrix products  45.4 us (16%)
  local copies, waits for them, and re-layouts  27 us (9%)
  between operations  15.9 us (6%)
  other arithmetic  13.3 us (5%)
  blocking collectives  9.95 us (3%)
    ppermute x14, waiting for transfers between devices, passed_along(): return lax.ppermute(x, axis, pairs)  69.3 us
    ppermute x14, starting transfers between devices, passed_along(): return lax.ppermute(x, axis, pairs)  65.6 us
    psum x1, waiting for transfers between devices, local(): lax.psum(kernel_stack.astype(jnp.bfloat16), 'dp').astype(jnp.float32)  40.4 us
    dot_general x81, matrix products, convolve(): jnp.dot(view, kernel[tap_index], preferred_element_type=jnp.float32)  18.1 us
    dot_general x72, matrix products, transposed(): lax.dot_general(view, kernel[tap_index], (((1,), (1,)), ((), ())), prefer...  17.6 us
    while x28, local copies, waits for them, and re-layouts  10.5 us
    psum x1, blocking collectives, local(): lax.psum(bias_stack.astype(jnp.bfloat16), 'dp').astype(jnp.float32)  9.95 us
    dot_general x36, matrix products, correlate(): lax.dot_general(view, flat_signal, (((0,), (0,)), ((), ())), preferred_el...  9.73 us
  transfers between devices with their start and end apart: 15, of which 15 were waited for; matrix products, arithmetic and copies ran while one was open for 2% of the time, Pallas kernels for 0%

commit v1 on v0

v1 whole, which is shorter than its diff:
```python
import functools
import math

import jax
import jax.numpy as jnp
from jax import lax
from jax.experimental import pallas as pl
from jax.experimental.pallas import tpu as pltpu
from jax.sharding import PartitionSpec as P

step_size = 0.25
MESH = pl.DeviceIdType.MESH
f32 = jnp.float32
bf16 = jnp.bfloat16


def kernel(
    cfg,
    starts, weights, biases, adj_ends,
    ends, adj_starts, wgrad, bgrad,
    a3f, a3s, slope, offs, ent, ext, txf, txb, wt, a3t, brow,
    gsend, grx, gred, bias_all,
    fsend, frecv, bsend, brecv, rs_send, rs_recv, ag_send, ag_recv, bi_send, bi_recv,
):
    blocks, peers, depth, side, chans, groups, bands, chunk = cfg
    pix = side * side
    pad = side
    taps = 9 * chans
    per_group = depth // groups
    group_rows = per_group * taps
    share = group_rows // peers
    coarse_step = depth * step_size
    grad_scale = 1.0 / (side * math.sqrt(peers))
    band = pix // bands

    k = lax.axis_index("layer")
    me = lax.axis_index("dp")
    first = k == 0
    last = k == blocks - 1
    peer = [lax.rem(me + d, peers) for d in range(1, peers)]

    barrier = pltpu.get_barrier_semaphore()

    @pl.when(jnp.logical_not(first))
    def _():
        pl.semaphore_signal(barrier, inc=1, device_id={"layer": k - 1}, device_id_type=MESH)

    @pl.when(jnp.logical_not(last))
    def _():
        pl.semaphore_signal(barrier, inc=1, device_id={"layer": k + 1}, device_id_type=MESH)

    for p in peer:
        pl.semaphore_signal(barrier, inc=1, device_id={"dp": p}, device_id_type=MESH)
    greeted = (peers - 1) + jnp.where(first, 0, 1) + jnp.where(last, 0, 1)

    def put3(dst, row, val):
        rows = val.shape[0]
        col = lax.rem(lax.broadcasted_iota(jnp.int32, (rows, chans), 0), side)
        before = jnp.where(col == 0, 0.0, pltpu.roll(val, 1, 0))
        after = jnp.where(col == side - 1, 0.0, pltpu.roll(val, rows - 1, 0))
        at = pl.ds(pad + row, rows)
        dst[at, 0:chans] = before.astype(bf16)
        dst[at, chans : 2 * chans] = val.astype(bf16)
        dst[at, 2 * chans : 3 * chans] = after.astype(bf16)

    def conv(src, row, rows, mat):
        lhs = jnp.concatenate([src[pl.ds(row + e * side, rows), :] for e in range(3)], axis=1)
        return jnp.dot(lhs, mat, preferred_element_type=f32)

    bias32 = biases[...].astype(f32)
    for i in range(depth):
        brow[i] = bias32[i : i + 1]
    zeros = jnp.zeros((pad, 3 * chans), bf16)
    for i in range(depth + 1):
        a3f[i, 0:pad] = zeros
        a3f[i, pad + pix : 2 * pad + pix] = zeros
    for i in range(2):
        a3s[i, 0:pad] = zeros
        a3s[i, pad + pix : 2 * pad + pix] = zeros

    chunks = list(range(0, pix, chunk))

    for r in chunks:
        put3(a3f.at[0], r, starts[r : r + chunk])
    for r in chunks:
        act = jnp.tanh(conv(a3f.at[0], r, chunk, weights[0]) + brow[0])
        slope[0, r : r + chunk] = 1.0 - act * act
        u0 = starts[r : r + chunk]
        u1 = u0 + step_size * act
        offs[r : r + chunk] = u0 + coarse_step * act
        ends[r : r + chunk] = u1
        put3(a3f.at[1], r, u1)

    def forward_layer(i, _):
        for r in chunks:
            act = jnp.tanh(conv(a3f.at[i], r, chunk, weights[i]) + brow[i])
            slope[i, r : r + chunk] = 1.0 - act * act
            u = ends[r : r + chunk] + step_size * act
            ends[r : r + chunk] = u
            put3(a3f.at[i + 1], r, u)
        return 0

    lax.fori_loop(1, depth, forward_layer, 0)
    for r in chunks:
        offs[r : r + chunk] = ends[r : r + chunk] - offs[r : r + chunk]

    def turn_weights():
        def one(i, _):
            for t in range(9):
                wt[i, t * chans : (t + 1) * chans] = weights[i, (8 - t) * chans : (9 - t) * chans].T
            return 0

        lax.fori_loop(0, depth, one, 0)

    def turn_states():
        def one(i, _):
            for d in range(3):
                for r in range(0, pix, chans):
                    a3t[i, d * chans : (d + 1) * chans, r : r + chans] = a3f[
                        i, pad + r : pad + r + chans, d * chans : (d + 1) * chans
                    ].T
            return 0

        lax.fori_loop(0, depth, one, 0)

    early = k < blocks // 2
    late = jnp.logical_not(early)
    pl.when(late)(turn_weights)

    pl.semaphore_wait(barrier, greeted)

    def hop(src, dst, send, recv, b, to):
        at = pl.ds(b * band, band)
        return pltpu.make_async_remote_copy(
            src_ref=src.at[at], dst_ref=dst.at[at], send_sem=send.at[b], recv_sem=recv.at[b],
            device_id={"layer": to}, device_id_type=MESH,
        )

    up = lax.rem(k + 1, blocks)
    down = lax.rem(k + blocks - 1, blocks)
    fwd = [hop(txf, ent, fsend, frecv, b, up) for b in range(bands)]
    bwd = [hop(txb, ext, bsend, brecv, b, down) for b in range(bands)]

    @pl.when(first)
    def _():
        for b in range(bands):
            at = pl.ds(b * band, band)
            txf[at] = ends[at].astype(bf16)
            fwd[b].start()

    @pl.when(jnp.logical_not(first))
    def _():
        def work(b):
            at = pl.ds(b * band, band)
            act = jnp.tanh(conv(a3f.at[0], b * band, band, weights[0]) + brow[0])
            state = ent[at].astype(f32)

            @pl.when(jnp.logical_not(last))
            def _():
                txf[at] = (offs[at] + (state + coarse_step * act)).astype(bf16)
                fwd[b].start()

            slope[0, at] = 1.0 - act * act
            u = state + step_size * act
            ends[at] = u
            put3(a3f.at[1], b * band, u)

        for b in range(bands):
            fwd[b].wait_recv()
            put3(a3f.at[0], b * band, ent[pl.ds(b * band, band)].astype(f32))
            if b:
                work(b - 1)
        work(bands - 1)
        lax.fori_loop(1, depth, forward_layer, 0)

    pl.when(early)(turn_weights)

    top = depth - 1
    for r in chunks:
        l = adj_ends[r : r + chunk]
        adj_starts[r : r + chunk] = l
        put3(a3s.at[top % 2], r, slope[top, r : r + chunk] * l)

    def adjoint_layer(i):
        now = lax.rem(i, 2)
        below = jnp.maximum(i - 1, 0)
        for r in chunks:
            l = adj_starts[r : r + chunk] + step_size * conv(a3s.at[now], r, chunk, wt[i])
            adj_starts[r : r + chunk] = l
            put3(a3s.at[1 - now], r, slope[below, r : r + chunk] * l)

    def back_layer(j, _):
        adjoint_layer(top - j)
        return 0

    lax.fori_loop(0, depth, back_layer, 0)

    @pl.when(last)
    def _():
        for b in range(bands):
            at = pl.ds(b * band, band)
            txb[at] = adj_starts[at].astype(bf16)
            bwd[b].start()

    pl.when(early)(turn_states)

    @pl.when(jnp.logical_not(last))
    def _():
        @pl.when(jnp.logical_not(first))
        def _():
            def work(b):
                at = pl.ds(b * band, band)
                diff = ext[at].astype(f32) - adj_ends[at]
                out = adj_starts[at] + (diff + coarse_step * conv(a3s.at[0], b * band, band, wt[0]))
                txb[at] = out.astype(bf16)
                bwd[b].start()

            for b in range(bands):
                at = pl.ds(b * band, band)
                bwd[b].wait_recv()
                put3(a3s.at[0], b * band, slope[0, at] * (ext[at].astype(f32) - adj_ends[at]))
                if b:
                    work(b - 1)
            work(bands - 1)

        @pl.when(first)
        def _():
            for b in range(bands):
                bwd[b].wait_recv()

        for r in chunks:
            adj_starts[r : r + chunk] = ext[r : r + chunk].astype(f32)

    @pl.when(last)
    def _():
        for r in chunks:
            adj_starts[r : r + chunk] = adj_ends[r : r + chunk]

    for r in chunks:
        put3(a3s.at[top % 2], r, slope[top, r : r + chunk] * adj_starts[r : r + chunk])
    pl.when(late)(turn_states)

    mine = pl.ds(pl.multiple_of(me * share, share), share)

    def scatter(g, d):
        theirs = pl.ds(pl.multiple_of(peer[d] * share, share), share)
        return pltpu.make_async_remote_copy(
            src_ref=gsend.at[g, theirs], dst_ref=grx.at[g, d],
            send_sem=rs_send.at[g, d], recv_sem=rs_recv.at[g, d],
            device_id={"dp": peer[d]}, device_id_type=MESH,
        )

    def gather(g, d):
        return pltpu.make_async_remote_copy(
            src_ref=gred.at[g, mine], dst_ref=gred.at[g, mine],
            send_sem=ag_send.at[g, d], recv_sem=ag_recv.at[g, d],
            device_id={"dp": peer[d]}, device_id_type=MESH,
        )

    def bias_copy(d):
        return pltpu.make_async_remote_copy(
            src_ref=bias_all.at[me], dst_ref=bias_all.at[me],
            send_sem=bi_send.at[d], recv_sem=bi_recv.at[d],
            device_id={"dp": peer[d]}, device_id_type=MESH,
        )

    def reduce_group(g):
        for d in range(peers - 1):
            scatter(g, d).wait_recv()
        total = gsend[g, mine].astype(f32)
        for d in range(peers - 1):
            total = total + grx[g, d].astype(f32)
        gred[g, mine] = total.astype(bf16)
        for d in range(peers - 1):
            gather(g, d).start()

    def final_group(j, _):
        g = groups - 1 - j
        for q in reversed(range(per_group)):
            i = g * per_group + q
            now = lax.rem(i, 2)
            sig = a3s.at[now]
            rhs = jnp.concatenate(
                [sig[(2 - e) * side : (2 - e) * side + pix, chans : 2 * chans] for e in range(3)], axis=1
            )
            found = jnp.dot(a3t[i], rhs, preferred_element_type=f32) * grad_scale
            for e in range(3):
                for d in range(3):
                    to = q * taps + (3 * e + d) * chans
                    gsend[g, to : to + chans] = found[
                        d * chans : (d + 1) * chans, e * chans : (e + 1) * chans
                    ].astype(bf16)
            summed = jnp.sum(sig[pad : pad + pix, chans : 2 * chans].astype(f32), axis=0, keepdims=True)
            brow[i] = summed * grad_scale
            if q == 0:
                for d in range(peers - 1):
                    scatter(g, d).start()
            adjoint_layer(i)

        @pl.when(j > 0)
        def _():
            reduce_group(jnp.minimum(g + 1, groups - 1))

        return 0

    lax.fori_loop(0, groups, final_group, 0)
    for i in range(depth):
        bias_all[me, i : i + 1] = brow[i]
    for d in range(peers - 1):
        bias_copy(d).start()
    reduce_group(0)

    for d in range(peers - 1):
        bias_copy(d).wait_recv()
    total = bias_all[0, 0:depth]
    for p in range(1, peers):
        total = total + bias_all[p, 0:depth]
    bgrad[...] = total

    def finish(j, _):
        g = groups - 1 - j
        for d in range(peers - 1):
            gather(g, d).wait_recv()
        for q in range(per_group):
            wgrad[g * per_group + q] = gred[g, q * taps : (q + 1) * taps].astype(f32)
        return 0

    lax.fori_loop(0, groups, finish, 0)

    @pl.when(jnp.logical_not(last))
    def _():
        for b in range(bands):
            fwd[b].wait_send()

    @pl.when(jnp.logical_not(first))
    def _():
        for b in range(bands):
            bwd[b].wait_send()

    def drain(g, _):
        for d in range(peers - 1):
            scatter(g, d).wait_send()
            gather(g, d).wait_send()
        return 0

    lax.fori_loop(0, groups, drain, 0)
    for d in range(peers - 1):
        bias_copy(d).wait_send()


def local(blocks, peers, starts, weights, biases, adj_ends):
    _, _, side, _, chans = starts.shape
    depth = weights.shape[0]
    pix = side * side
    taps = 9 * chans
    bands = 4
    chunk = min(256, pix)
    groups = max(
        g for g in range(1, depth + 1)
        if depth % g == 0 and (depth // g * taps) % (16 * peers) == 0
    )
    group_rows = depth // groups * taps
    share = group_rows // peers
    cfg = (blocks, peers, depth, side, chans, groups, bands, chunk)
    padded = pix + 2 * side
    vmem = pl.BlockSpec(memory_space=pltpu.VMEM)
    dma = pltpu.SemaphoreType.DMA
    others = peers - 1
    outs = pl.pallas_call(
        functools.partial(kernel, cfg),
        out_shape=(
            jax.ShapeDtypeStruct((pix, chans), f32),
            jax.ShapeDtypeStruct((pix, chans), f32),
            jax.ShapeDtypeStruct((depth, taps, chans), f32),
            jax.ShapeDtypeStruct((depth, chans), f32),
        ),
        in_specs=[vmem] * 4,
        out_specs=(vmem,) * 4,
        scratch_shapes=[
            pltpu.VMEM((depth + 1, padded, 3 * chans), bf16),
            pltpu.VMEM((2, padded, 3 * chans), bf16),
            pltpu.VMEM((depth, pix, chans), f32),
            pltpu.VMEM((pix, chans), f32),
            pltpu.VMEM((pix, chans), bf16),
            pltpu.VMEM((pix, chans), bf16),
            pltpu.VMEM((pix, chans), bf16),
            pltpu.VMEM((pix, chans), bf16),
            pltpu.VMEM((depth, taps, chans), bf16),
            pltpu.VMEM((depth, 3 * chans, pix), bf16),
            pltpu.VMEM((depth, 1, chans), f32),
            pltpu.VMEM((groups, group_rows, chans), bf16),
            pltpu.VMEM((groups, others, share, chans), bf16),
            pltpu.VMEM((groups, group_rows, chans), bf16),
            pltpu.VMEM((peers, -(-depth // 8) * 8, chans), f32),
            dma((bands,)), dma((bands,)), dma((bands,)), dma((bands,)),
            dma((groups, others)), dma((groups, others)),
            dma((groups, others)), dma((groups, others)),
            dma((others,)), dma((others,)),
        ],
        compiler_params=pltpu.CompilerParams(
            collective_id=0, has_side_effects=True, vmem_limit_bytes=56 * 1024 * 1024
        ),
    )(
        starts.reshape(pix, chans), weights.reshape(depth, taps, chans), biases,
        adj_ends.reshape(pix, chans),
    )
    ends, adj_starts, wgrad, bgrad = outs
    return (
        ends.reshape(starts.shape), adj_starts.reshape(starts.shape),
        wgrad.reshape(weights.shape), bgrad,
    )


def solution(mesh):
    in_specs = (
        P("layer", "dp", None, None, None),
        P("layer", None, None, None),
        P("layer", None),
        P("layer", "dp", None, None, None),
    )
    out_specs = (
        P("layer", "dp", None, None, None),
        P("layer", "dp", None, None, None),
        P("layer", None, None, None),
        P("layer", None),
    )
    run = functools.partial(local, mesh.shape["layer"], mesh.shape["dp"])
    return jax.shard_map(run, mesh=mesh, in_specs=in_specs, out_specs=out_specs, check_vma=False)
```

time: 289 us -> 93.9 us (0.32)
  waiting for transfers between devices: 110 us -> 0 us
  Pallas kernels: 0 us -> 85.3 us
  starting transfers between devices: 65.7 us -> 0 us
  matrix products: 45.4 us -> 0 us
  local copies, waits for them, and re-layouts: 27 us -> 7.64 us
  between operations: 15.9 us -> 0.64 us
  other arithmetic: 13.3 us -> 0 us
  blocking collectives: 9.95 us -> 0 us
    pallas_call x0 -> x1, Pallas kernels: none -> 85.3 us  [local(): pl.pallas_call(functools.partial(kernel, cfg), out_shape=(jax.ShapeDtypeS...]
    ppermute x14 -> x0, waiting for transfers between devices: 69.3 us -> none  [passed_along(): return lax.ppermute(x, axis, pairs)]
    ppermute x14 -> x0, starting transfers between devices: 65.6 us -> none  [passed_along(): return lax.ppermute(x, axis, pairs)]
    dot_general x189 -> x0, matrix products: 45.4 us -> none  [the longest x81 18.1 us: convolve(): jnp.dot(view, kernel[tap_index], preferred_element_type=jnp.float32)]
    psum x1 -> x0, waiting for transfers between devices: 40.4 us -> none  [local(): lax.psum(kernel_stack.astype(jnp.bfloat16), 'dp').astype(jnp.float32)]
    while x28 -> x0, local copies, waits for them, and re-layouts: 10.5 us -> none
    psum x1 -> x0, blocking collectives: 9.95 us -> none  [local(): lax.psum(bias_stack.astype(jnp.bfloat16), 'dp').astype(jnp.float32)]
    slice x17 -> x0, local copies, waits for them, and re-layouts: 7.17 us -> none  [the longest x9 3.64 us: convolve(): padded[:, row_off:row_off + map_side, col_off:col_off + map_side, :]]
  transfers between devices with their start and end apart: 15 -> 0, of which waited for: 15 -> 0; matrix products, arithmetic and copies ran while one was open for 2% -> 0% of each run, Pallas kernels for 0% -> 0%
where the time goes in v1:
time: 93.9 us; the launch traced here: 93.6 us
  Pallas kernels  85.3 us (91%)
  local copies, waits for them, and re-layouts  7.64 us (8%)
    pallas_call x1, Pallas kernels, local(): pl.pallas_call(functools.partial(kernel, cfg), out_shape=(jax.ShapeDtypeS...  85.3 us
    unnamed x6, local copies, waits for them, and re-layouts  7.64 us

profile of v1, /device:TPU:0, one launch (start us, length us, event | category | flops | bytes accessed | tf_op | source)
XLA Modules:
  0.0 93.6 jit_solution(12734936504555065886)
XLA Ops:
  0.6 85.3 %shard_map.75 = (f32[1024,128]{1,0:T(8,128)}, f32[1024,128]{1,0:T(8,128)}, f32[4,1152,128]{2,1,0:T(8,128)}, f32[4,128]{1,0:T(4,128)}) custom-call(f32[1024,128]{1,0:T(8,128)} %bitcast.10, bf16[4,1152,128]{2,1,0:T(8,128)(2,1)} %bitcast.7, bf16[4,128]{1,0:T(4,128)(2,1)} %biases.1, f32[1024,128]{1,0:T(8,128)} %bitcast.11), custom_call_target="tpu_custom_call" | custom-call | tf_op jit(solution)/shard_map/pallas_call | solution.py:369
  86.0 1.9 %copy.12 = f32[1,1,32,32,128]{4,3,2,1,0:T(8,128)} copy(f32[1,1,32,32,128]{4,3,2,1,0:T(8,128)} %bitcast.9) | data formatting | bytes 1048576
  87.9 1.9 %copy.13 = f32[1,1,32,32,128]{4,3,2,1,0:T(8,128)} copy(f32[1,1,32,32,128]{4,3,2,1,0:T(8,128)} %bitcast.8) | data formatting | bytes 1048576
  89.7 0.0 copy-start
  89.7 3.3 %copy.14 = f32[4,9,128,128]{3,2,1,0:T(8,128)} copy(f32[4,9,128,128]{3,2,1,0:T(8,128)} %bitcast.6) | data formatting | bytes 4718592
  93.0 0.0 copy-done
  93.1 0.6 copy.15
Async XLA Ops:
  89.7 3.3 %copy-start = (f32[4,128]{1,0:T(4,128)S(1)}, f32[4,128]{1,0:T(4,128)}, u32[]{:S(2)}) copy-start(f32[4,128]{1,0:T(4,128)} %get-tuple-element.19) | copy-start | bytes 6148

commit v2 on v1

--- a/solution.py
+++ b/solution.py
@@ -17,18 +17,21 @@
 def kernel(
     cfg,
     starts, weights, biases, adj_ends,
-    ends, adj_starts, wgrad, bgrad,
-    a3f, a3s, slope, offs, ent, ext, txf, txb, wt, a3t, brow,
-    gsend, grx, gred, bias_all,
-    fsend, frecv, bsend, brecv, rs_send, rs_recv, ag_send, ag_recv, bi_send, bi_recv,
+    ends_out, adj_out, wgrad_out, bgrad,
+    ends, adj_starts, a3f, a3s, slope, offs, ent, ext, txf, txb, wt, a3t, brow,
+    gsend, rx1, mid, rx2, gred, bias_all,
+    fsend, frecv, bsend, brecv, one_send, one_recv, two_send, two_recv,
+    three_send, three_recv, four_send, four_recv, bi_send, bi_recv, out_sem,
 ):
-    blocks, peers, depth, side, chans, groups, bands, chunk = cfg
+    blocks, peers, lows, depth, side, chans, groups, bands, chunk = cfg
+    highs = peers // lows
     pix = side * side
     pad = side
     taps = 9 * chans
     per_group = depth // groups
     group_rows = per_group * taps
-    share = group_rows // peers
+    half = group_rows // 2
+    share = half // peers
     coarse_step = depth * step_size
     grad_scale = 1.0 / (side * math.sqrt(peers))
     band = pix // bands
@@ -173,6 +176,8 @@
         work(bands - 1)
         lax.fori_loop(1, depth, forward_layer, 0)
 
+    ends_copy = pltpu.make_async_copy(ends, ends_out, out_sem.at[0])
+    ends_copy.start()
     pl.when(early)(turn_weights)
 
     top = depth - 1
@@ -240,22 +245,93 @@
         put3(a3s.at[top % 2], r, slope[top, r : r + chunk] * adj_starts[r : r + chunk])
     pl.when(late)(turn_states)
 
-    mine = pl.ds(pl.multiple_of(me * share, share), share)
-
-    def scatter(g, d):
-        theirs = pl.ds(pl.multiple_of(peer[d] * share, share), share)
+    high, low = me // lows, lax.rem(me, lows)
+    counts = ((lows, highs), (highs, lows))
+    spots = ((low, high), (high, low))
+
+    def turned(h, stage, d):
+        c = list(spots[h])
+        c[stage] = lax.rem(c[stage] + d + 1, counts[h][stage])
+        return c
+
+    def number(h, c):
+        return c[1] * lows + c[0] if h == 0 else c[0] * lows + c[1]
+
+    def wide(h, c):
+        rows = half // counts[h][0]
+        return pl.ds(pl.multiple_of(h * half + c[0] * rows, 16), rows)
+
+    def narrow(h, c):
+        rows = half // counts[h][0]
+        return pl.ds(pl.multiple_of(h * half + c[0] * rows + c[1] * share, 16), share)
+
+    def send(src, dst, ssem, rsem, to):
         return pltpu.make_async_remote_copy(
-            src_ref=gsend.at[g, theirs], dst_ref=grx.at[g, d],
-            send_sem=rs_send.at[g, d], recv_sem=rs_recv.at[g, d],
-            device_id={"dp": peer[d]}, device_id_type=MESH,
+            src_ref=src, dst_ref=dst, send_sem=ssem, recv_sem=rsem,
+            device_id={"dp": to}, device_id_type=MESH,
         )
 
-    def gather(g, d):
-        return pltpu.make_async_remote_copy(
-            src_ref=gred.at[g, mine], dst_ref=gred.at[g, mine],
-            send_sem=ag_send.at[g, d], recv_sem=ag_recv.at[g, d],
-            device_id={"dp": peer[d]}, device_id_type=MESH,
-        )
+    def one(g, h):
+        rows = pl.ds(0, half // counts[h][0])
+        for d in range(counts[h][0] - 1):
+            c = turned(h, 0, d)
+            yield send(gsend.at[g, wide(h, c)], rx1.at[g, h, d, rows],
+                       one_send.at[g, h, d], one_recv.at[g, h, d], number(h, c))
+
+    def two(g, h):
+        for d in range(counts[h][1] - 1):
+            c = turned(h, 1, d)
+            src = pl.ds(pl.multiple_of(c[1] * share, 16), share)
+            yield send(mid.at[g, h, src], rx2.at[g, h, d],
+                       two_send.at[g, h, d], two_recv.at[g, h, d], number(h, c))
+
+    def three(g, h):
+        at = narrow(h, spots[h])
+        for d in range(counts[h][1] - 1):
+            yield send(gred.at[g, at], gred.at[g, at],
+                       three_send.at[g, h, d], three_recv.at[g, h, d], number(h, turned(h, 1, d)))
+
+    def four(g, h):
+        at = wide(h, spots[h])
+        for d in range(counts[h][0] - 1):
+            yield send(gred.at[g, at], gred.at[g, at],
+                       four_send.at[g, h, d], four_recv.at[g, h, d], number(h, turned(h, 0, d)))
+
+    def start_one(g):
+        for h in range(2):
+            for c in one(g, h):
+                c.start()
+
+    def start_two(g):
+        for h in range(2):
+            for c in one(g, h):
+                c.wait_recv()
+            rows = half // counts[h][0]
+            total = gsend[g, wide(h, spots[h])].astype(f32)
+            for d in range(counts[h][0] - 1):
+                total = total + rx1[g, h, d, 0:rows].astype(f32)
+            mid[g, h, 0:rows] = total.astype(bf16)
+            for c in two(g, h):
+                c.start()
+
+    def start_three(g):
+        for h in range(2):
+            for c in two(g, h):
+                c.wait_recv()
+            own = pl.ds(pl.multiple_of(spots[h][1] * share, 16), share)
+            total = mid[g, h, own].astype(f32)
+            for d in range(counts[h][1] - 1):
+                total = total + rx2[g, h, d].astype(f32)
+            gred[g, narrow(h, spots[h])] = total.astype(bf16)
+            for c in three(g, h):
+                c.start()
+
+    def start_four(g):
+        for h in range(2):
+            for c in three(g, h):
+                c.wait_recv()
+            for c in four(g, h):
+                c.start()
 
     def bias_copy(d):
         return pltpu.make_async_remote_copy(
@@ -263,16 +339,6 @@
             send_sem=bi_send.at[d], recv_sem=bi_recv.at[d],
             device_id={"dp": peer[d]}, device_id_type=MESH,
         )
-
-    def reduce_group(g):
-        for d in range(peers - 1):
-            scatter(g, d).wait_recv()
-        total = gsend[g, mine].astype(f32)
-        for d in range(peers - 1):
-            total = total + grx[g, d].astype(f32)
-        gred[g, mine] = total.astype(bf16)
-        for d in range(peers - 1):
-            gather(g, d).start()
 
     def final_group(j, _):
         g = groups - 1 - j
@@ -293,22 +359,28 @@
             summed = jnp.sum(sig[pad : pad + pix, chans : 2 * chans].astype(f32), axis=0, keepdims=True)
             brow[i] = summed * grad_scale
             if q == 0:
-                for d in range(peers - 1):
-                    scatter(g, d).start()
+                start_one(g)
             adjoint_layer(i)
 
-        @pl.when(j > 0)
-        def _():
-            reduce_group(jnp.minimum(g + 1, groups - 1))
+        for lag, stage in ((3, start_four), (2, start_three), (1, start_two)):
+            @pl.when(j >= lag)
+            def _():
+                stage(jnp.minimum(g + lag, groups - 1))
 
         return 0
 
     lax.fori_loop(0, groups, final_group, 0)
     for i in range(depth):
         bias_all[me, i : i + 1] = brow[i]
+    adj_copy = pltpu.make_async_copy(adj_starts, adj_out, out_sem.at[1])
+    adj_copy.start()
     for d in range(peers - 1):
         bias_copy(d).start()
-    reduce_group(0)
+    for step in range(3):
+        for lag, stage in ((3, start_four), (2, start_three), (1, start_two)):
+            j = groups + step - lag
+            if 0 <= j < groups:
+                stage(groups - 1 - j)
 
     for d in range(peers - 1):
         bias_copy(d).wait_recv()
@@ -317,12 +389,15 @@
         total = total + bias_all[p, 0:depth]
     bgrad[...] = total
 
+    def grad_copy(g):
+        return pltpu.make_async_copy(gred.at[g], wgrad_out.at[g], out_sem.at[2 + g])
+
     def finish(j, _):
         g = groups - 1 - j
-        for d in range(peers - 1):
-            gather(g, d).wait_recv()
-        for q in range(per_group):
-            wgrad[g * per_group + q] = gred[g, q * taps : (q + 1) * taps].astype(f32)
+        for h in range(2):
+            for c in four(g, h):
+                c.wait_recv()
+        grad_copy(g).start()
         return 0
 
     lax.fori_loop(0, groups, finish, 0)
@@ -338,14 +413,25 @@
             bwd[b].wait_send()
 
     def drain(g, _):
-        for d in range(peers - 1):
-            scatter(g, d).wait_send()
-            gather(g, d).wait_send()
+        for h in range(2):
+            for stage in (one, two, three, four):
+                for c in stage(g, h):
+                    c.wait_send()
+        grad_copy(g).wait()
         return 0
 
     lax.fori_loop(0, groups, drain, 0)
     for d in range(peers - 1):
         bias_copy(d).wait_send()
+    ends_copy.wait()
+    adj_copy.wait()
+
+
+def unpack(ends, adj_starts, wgrad, bgrad, ends_out, adj_out, wgrad_out, bgrad_out):
+    ends_out[...] = ends[...]
+    adj_out[...] = adj_starts[...]
+    wgrad_out[...] = wgrad[...].astype(f32)
+    bgrad_out[...] = bgrad[...]
 
 
 def local(blocks, peers, starts, weights, biases, adj_ends):
@@ -353,17 +439,21 @@
     depth = weights.shape[0]
     pix = side * side
     taps = 9 * chans
-    bands = 4
+    bands = 8
     chunk = min(256, pix)
+    lows = min(n for n in range(1, peers + 1) if peers % n == 0 and n * n >= peers)
+    highs = peers // lows
     groups = max(
         g for g in range(1, depth + 1)
-        if depth % g == 0 and (depth // g * taps) % (16 * peers) == 0
+        if depth % g == 0 and (depth // g * taps) % (32 * peers) == 0
     )
     group_rows = depth // groups * taps
-    share = group_rows // peers
-    cfg = (blocks, peers, depth, side, chans, groups, bands, chunk)
+    half = group_rows // 2
+    slots = max(1, lows - 1, highs - 1)
+    cfg = (blocks, peers, lows, depth, side, chans, groups, bands, chunk)
     padded = pix + 2 * side
     vmem = pl.BlockSpec(memory_space=pltpu.VMEM)
+    anywhere = pl.BlockSpec(memory_space=pl.ANY)
     dma = pltpu.SemaphoreType.DMA
     others = peers - 1
     outs = pl.pallas_call(
@@ -371,12 +461,14 @@
         out_shape=(
             jax.ShapeDtypeStruct((pix, chans), f32),
             jax.ShapeDtypeStruct((pix, chans), f32),
-            jax.ShapeDtypeStruct((depth, taps, chans), f32),
+            jax.ShapeDtypeStruct((groups, group_rows, chans), bf16),
             jax.ShapeDtypeStruct((depth, chans), f32),
         ),
         in_specs=[vmem] * 4,
-        out_specs=(vmem,) * 4,
+        out_specs=(anywhere, anywhere, anywhere, vmem),
         scratch_shapes=[
+            pltpu.VMEM((pix, chans), f32),
+            pltpu.VMEM((pix, chans), f32),
             pltpu.VMEM((depth + 1, padded, 3 * chans), bf16),
             pltpu.VMEM((2, padded, 3 * chans), bf16),
             pltpu.VMEM((depth, pix, chans), f32),
@@ -389,13 +481,15 @@
             pltpu.VMEM((depth, 3 * chans, pix), bf16),
             pltpu.VMEM((depth, 1, chans), f32),
             pltpu.VMEM((groups, group_rows, chans), bf16),
-            pltpu.VMEM((groups, others, share, chans), bf16),
+            pltpu.VMEM((groups, 2, slots, half // min(lows, highs), chans), bf16),
+            pltpu.VMEM((groups, 2, half // min(lows, highs), chans), bf16),
+            pltpu.VMEM((groups, 2, slots, half // peers, chans), bf16),
             pltpu.VMEM((groups, group_rows, chans), bf16),
             pltpu.VMEM((peers, -(-depth // 8) * 8, chans), f32),
             dma((bands,)), dma((bands,)), dma((bands,)), dma((bands,)),
-            dma((groups, others)), dma((groups, others)),
-            dma((groups, others)), dma((groups, others)),
-            dma((others,)), dma((others,)),
+            *[dma((groups, 2, slots))] * 8,
+            dma((max(1, others),)), dma((max(1, others),)),
+            dma((2 + groups,)),
         ],
         compiler_params=pltpu.CompilerParams(
             collective_id=0, has_side_effects=True, vmem_limit_bytes=56 * 1024 * 1024
@@ -404,7 +498,19 @@
         starts.reshape(pix, chans), weights.reshape(depth, taps, chans), biases,
         adj_ends.reshape(pix, chans),
     )
-    ends, adj_starts, wgrad, bgrad = outs
+    rows = pix // groups
+    part = pl.BlockSpec((rows, chans), lambda g: (g, 0))
+    block = pl.BlockSpec((1, group_rows, chans), lambda g: (g, 0, 0))
+    whole = pl.BlockSpec((depth, chans), lambda g: (0, 0))
+    specs = (part, part, block, whole)
+    ends, adj_starts, wgrad, bgrad = pl.pallas_call(
+        unpack,
+        grid=(groups,),
+        out_shape=tuple(jax.ShapeDtypeStruct(o.shape, f32) for o in outs),
+        in_specs=list(specs),
+        out_specs=specs,
+        compiler_params=pltpu.CompilerParams(vmem_limit_bytes=32 * 1024 * 1024),
+    )(*outs)
     return (
         ends.reshape(starts.shape), adj_starts.reshape(starts.shape),
         wgrad.reshape(weights.shape), bgrad,

time: 93.9 us -> 85.9 us (0.915)
  Pallas kernels: 85.3 us -> 80.9 us
  local copies, waits for them, and re-layouts: 7.64 us -> 4.03 us
    pallas_call x1, Pallas kernels: 85.3 us -> 78.7 us  [local(): pl.pallas_call(functools.partial(kernel, cfg), out_shape=(jax.ShapeDtypeS...]
    unnamed x6 -> x8, local copies, waits for them, and re-layouts: 7.64 us -> 4.03 us
    pallas_call x0 -> x1, Pallas kernels: none -> 2.17 us  [local(): pl.pallas_call(unpack, grid=(groups,), out_shape=tuple((jax.ShapeDtypeStr...]
where the time goes in v2:
time: 85.9 us; the launch traced here: 85.5 us
  Pallas kernels  80.9 us (94%)
  local copies, waits for them, and re-layouts  4.03 us (5%)
    pallas_call x1, Pallas kernels, local(): pl.pallas_call(functools.partial(kernel, cfg), out_shape=(jax.ShapeDtypeS...  78.7 us
    unnamed x8, local copies, waits for them, and re-layouts  4.03 us
    pallas_call x1, Pallas kernels, local(): pl.pallas_call(unpack, grid=(groups,), out_shape=tuple((jax.ShapeDtypeStr...  2.17 us

profile of v2, /device:TPU:0, one launch (start us, length us, event | category | flops | bytes accessed | tf_op | source)
XLA Modules:
  0.0 85.5 jit_solution(7754324181112639139)
XLA Ops:
  0.6 78.7 %shard_map.75 = (f32[1024,128]{1,0:T(8,128)}, f32[1024,128]{1,0:T(8,128)}, bf16[4,1152,128]{2,1,0:T(8,128)(2,1)}, f32[4,128]{1,0:T(4,128)}) custom-call(f32[1024,128]{1,0:T(8,128)} %bitcast.7, bf16[4,1152,128]{2,1,0:T(8,128)(2,1)} %bitcast.6, bf16[4,128]{1,0:T(4,128)(2,1)} %biases.1, f32[1024,128]{1,0:T(8,128)} %bitcast.8), custom_call_target="tpu_custom_call" | custom-call | tf_op jit(solution)/shard_map/pallas_call | solution.py:459
  79.3 0.0 copy-start
  79.3 1.3 %copy-done = bf16[4,1152,128]{2,1,0:T(8,128)(2,1)S(1)} copy-done((bf16[4,1152,128]{2,1,0:T(8,128)(2,1)S(1)}, bf16[4,1152,128]{2,1,0:T(8,128)(2,1)}, u32[]{:S(2)}) %copy-start) | copy-done | bytes 1179672
  80.6 0.0 copy-start.1
  80.6 1.0 %copy-done.1 = f32[1024,128]{1,0:T(8,128)S(1)} copy-done((f32[1024,128]{1,0:T(8,128)S(1)}, f32[1024,128]{1,0:T(8,128)}, u32[]{:S(2)}) %copy-start.1) | copy-done | bytes 524312
  81.7 0.0 copy-start.2
  81.7 1.0 %copy-done.2 = f32[1024,128]{1,0:T(8,128)S(1)} copy-done((f32[1024,128]{1,0:T(8,128)S(1)}, f32[1024,128]{1,0:T(8,128)}, u32[]{:S(2)}) %copy-start.2) | copy-done | bytes 524312
  82.7 0.0 copy-start.3
  82.7 0.7 copy-done.3
  83.4 2.2 %shard_map.76 = (f32[1024,128]{1,0:T(8,128)}, f32[1024,128]{1,0:T(8,128)}, f32[4,1152,128]{2,1,0:T(8,128)}, f32[4,128]{1,0:T(4,128)}) custom-call(f32[1024,128]{1,0:T(8,128)S(1)} %copy-done.1, f32[1024,128]{1,0:T(8,128)S(1)} %copy-done.2, bf16[4,1152,128]{2,1,0:T(8,128)(2,1)S(1)} %copy-done, f32[4,128]{1,0:T(4,128)S(1)} %copy-done.3), custom_call_target="tpu_custom_call" | custom-call | tf_op jit(solution)/shard_map/pallas_call | solution.py:506
Async XLA Ops:
  79.3 1.3 %copy-start = (bf16[4,1152,128]{2,1,0:T(8,128)(2,1)S(1)}, bf16[4,1152,128]{2,1,0:T(8,128)(2,1)}, u32[]{:S(2)}) copy-start(bf16[4,1152,128]{2,1,0:T(8,128)(2,1)} %get-tuple-element.14.wgrad) | copy-start | bytes 3538948
  80.6 1.0 %copy-start.1 = (f32[1024,128]{1,0:T(8,128)S(1)}, f32[1024,128]{1,0:T(8,128)}, u32[]{:S(2)}) copy-start(f32[1024,128]{1,0:T(8,128)} %get-tuple-element.12.ends) | copy-start | bytes 1572868
  81.7 1.0 %copy-start.2 = (f32[1024,128]{1,0:T(8,128)S(1)}, f32[1024,128]{1,0:T(8,128)}, u32[]{:S(2)}) copy-start(f32[1024,128]{1,0:T(8,128)} %get-tuple-element.13.adj_starts) | copy-start | bytes 1572868
  82.7 0.7 copy-start.3

commit v3 on v2

--- a/solution.py
+++ b/solution.py
@@ -32,6 +32,7 @@
     group_rows = per_group * taps
     half = group_rows // 2
     share = half // peers
+    top = depth - 1
     coarse_step = depth * step_size
     grad_scale = 1.0 / (side * math.sqrt(peers))
     band = pix // bands
@@ -74,7 +75,7 @@
     for i in range(depth):
         brow[i] = bias32[i : i + 1]
     zeros = jnp.zeros((pad, 3 * chans), bf16)
-    for i in range(depth + 1):
+    for i in range(depth):
         a3f[i, 0:pad] = zeros
         a3f[i, pad + pix : 2 * pad + pix] = zeros
     for i in range(2):
@@ -92,18 +93,20 @@
         u1 = u0 + step_size * act
         offs[r : r + chunk] = u0 + coarse_step * act
         ends[r : r + chunk] = u1
-        put3(a3f.at[1], r, u1)
-
-    def forward_layer(i, _):
+        if top:
+            put3(a3f.at[1], r, u1)
+
+    def forward_layer(i):
         for r in chunks:
             act = jnp.tanh(conv(a3f.at[i], r, chunk, weights[i]) + brow[i])
             slope[i, r : r + chunk] = 1.0 - act * act
             u = ends[r : r + chunk] + step_size * act
             ends[r : r + chunk] = u
-            put3(a3f.at[i + 1], r, u)
-        return 0
-
-    lax.fori_loop(1, depth, forward_layer, 0)
+            if i < top:
+                put3(a3f.at[i + 1], r, u)
+
+    for i in range(1, depth):
+        forward_layer(i)
     for r in chunks:
         offs[r : r + chunk] = ends[r : r + chunk] - offs[r : r + chunk]
 
@@ -166,7 +169,8 @@
             slope[0, at] = 1.0 - act * act
             u = state + step_size * act
             ends[at] = u
-            put3(a3f.at[1], b * band, u)
+            if top:
+                put3(a3f.at[1], b * band, u)
 
         for b in range(bands):
             fwd[b].wait_recv()
@@ -174,31 +178,28 @@
             if b:
                 work(b - 1)
         work(bands - 1)
-        lax.fori_loop(1, depth, forward_layer, 0)
+        for i in range(1, depth):
+            forward_layer(i)
 
     ends_copy = pltpu.make_async_copy(ends, ends_out, out_sem.at[0])
     ends_copy.start()
     pl.when(early)(turn_weights)
 
-    top = depth - 1
     for r in chunks:
         l = adj_ends[r : r + chunk]
         adj_starts[r : r + chunk] = l
         put3(a3s.at[top % 2], r, slope[top, r : r + chunk] * l)
 
     def adjoint_layer(i):
-        now = lax.rem(i, 2)
-        below = jnp.maximum(i - 1, 0)
+        now = i % 2
         for r in chunks:
             l = adj_starts[r : r + chunk] + step_size * conv(a3s.at[now], r, chunk, wt[i])
             adj_starts[r : r + chunk] = l
-            put3(a3s.at[1 - now], r, slope[below, r : r + chunk] * l)
-
-    def back_layer(j, _):
-        adjoint_layer(top - j)
-        return 0
-
-    lax.fori_loop(0, depth, back_layer, 0)
+            if i:
+                put3(a3s.at[1 - now], r, slope[i - 1, r : r + chunk] * l)
+
+    for i in reversed(range(depth)):
+        adjoint_layer(i)
 
     @pl.when(last)
     def _():
@@ -340,12 +341,11 @@
             device_id={"dp": peer[d]}, device_id_type=MESH,
         )
 
-    def final_group(j, _):
+    for j in range(groups):
         g = groups - 1 - j
         for q in reversed(range(per_group)):
             i = g * per_group + q
-            now = lax.rem(i, 2)
-            sig = a3s.at[now]
+            sig = a3s.at[i % 2]
             rhs = jnp.concatenate(
                 [sig[(2 - e) * side : (2 - e) * side + pix, chans : 2 * chans] for e in range(3)], axis=1
             )
@@ -363,13 +363,9 @@
             adjoint_layer(i)
 
         for lag, stage in ((3, start_four), (2, start_three), (1, start_two)):
-            @pl.when(j >= lag)
-            def _():
-                stage(jnp.minimum(g + lag, groups - 1))
-
-        return 0
-
-    lax.fori_loop(0, groups, final_group, 0)
+            if j >= lag:
+                stage(g + lag)
+
     for i in range(depth):
         bias_all[me, i : i + 1] = brow[i]
     adj_copy = pltpu.make_async_copy(adj_starts, adj_out, out_sem.at[1])
@@ -469,7 +465,7 @@
         scratch_shapes=[
             pltpu.VMEM((pix, chans), f32),
             pltpu.VMEM((pix, chans), f32),
-            pltpu.VMEM((depth + 1, padded, 3 * chans), bf16),
+            pltpu.VMEM((depth, padded, 3 * chans), bf16),
             pltpu.VMEM((2, padded, 3 * chans), bf16),
             pltpu.VMEM((depth, pix, chans), f32),
             pltpu.VMEM((pix, chans), f32),
@@ -509,7 +505,7 @@
         out_shape=tuple(jax.ShapeDtypeStruct(o.shape, f32) for o in outs),
         in_specs=list(specs),
         out_specs=specs,
-        compiler_params=pltpu.CompilerParams(vmem_limit_bytes=32 * 1024 * 1024),
+        compiler_params=pltpu.CompilerParams(vmem_limit_bytes=60 * 1024 * 1024),
     )(*outs)
     return (
         ends.reshape(starts.shape), adj_starts.reshape(starts.shape),

time: 85.9 us -> 80.8 us (0.941)
  local copies, waits for them, and re-layouts: 4.03 us -> 0 us
  Pallas kernels: 80.9 us -> 79.9 us
    unnamed x8 -> x0, local copies, waits for them, and re-layouts: 4.03 us -> none
    pallas_call x1, Pallas kernels: 78.7 us -> 75.8 us  [local(): pl.pallas_call(functools.partial(kernel, cfg), out_shape=(jax.ShapeDtypeS...]
    pallas_call x1, Pallas kernels: 2.17 us -> 4.1 us  [local(): pl.pallas_call(unpack, grid=(groups,), out_shape=tuple((jax.ShapeDtypeStr...]
where the time goes in v3:
time: 80.8 us; the launch traced here: 80.6 us
  Pallas kernels  79.9 us (99%)
    pallas_call x1, Pallas kernels, local(): pl.pallas_call(functools.partial(kernel, cfg), out_shape=(jax.ShapeDtypeS...  75.8 us
    pallas_call x1, Pallas kernels, local(): pl.pallas_call(unpack, grid=(groups,), out_shape=tuple((jax.ShapeDtypeStr...  4.1 us

profile of v3, /device:TPU:0, one launch (start us, length us, event | category | flops | bytes accessed | tf_op | source)
XLA Modules:
  0.0 80.6 jit_solution(17717653621092247238)
XLA Ops:
  0.6 75.8 %shard_map.75 = (f32[1024,128]{1,0:T(8,128)}, f32[1024,128]{1,0:T(8,128)}, bf16[4,1152,128]{2,1,0:T(8,128)(2,1)}, f32[4,128]{1,0:T(4,128)}) custom-call(f32[1024,128]{1,0:T(8,128)} %bitcast.7, bf16[4,1152,128]{2,1,0:T(8,128)(2,1)} %bitcast.6, bf16[4,128]{1,0:T(4,128)(2,1)} %biases.1, f32[1024,128]{1,0:T(8,128)} %bitcast.8), custom_call_target="tpu_custom_call" | custom-call | tf_op jit(solution)/shard_map/pallas_call | solution.py:455
  76.5 4.1 %shard_map.76 = (f32[1024,128]{1,0:T(8,128)}, f32[1024,128]{1,0:T(8,128)}, f32[4,1152,128]{2,1,0:T(8,128)}, f32[4,128]{1,0:T(4,128)}) custom-call(f32[1024,128]{1,0:T(8,128)} %get-tuple-element.12.ends, f32[1024,128]{1,0:T(8,128)} %get-tuple-element.13.adj_starts, bf16[4,1152,128]{2,1,0:T(8,128)(2,1)} %get-tuple-element.14.wgrad, ...), custom_call_target="tpu_custom_call" | custom-call | tf_op jit(solution)/shard_map/pallas_call | solution.py:502
